TPU v7x, 32 devices: a whole 2x2x4 slice. The times are simulated.
32 devices in a mesh: genome: 8 (over z, x), samp: 4 (over y, core).
Axes of the slice: x: 2, y: 2, z: 4, core: 2. Of those that a mesh axis runs over, the one named last changes fastest.
Arguments:
- dosage: bfloat16 [16384, 8192], P('samp', 'genome'), may hold values from -6 to 6
- effects: bfloat16 [8192, 512], P('genome', 'samp'), may hold values from -6 to 6
- depth: int32 [32], P('genome'), may hold values from 1 to 4
Outputs:
- ld_effects: float32 [8192, 512], P('genome', 'samp')
Inputs may be any that keep to these rules, and one draw needn't show every extreme that they name: Every block's window depth lies between 1 and 4.
All inputs are finite; a program needn't handle non-finite values.
Results may differ from a plain program's by a relative error of at most 0.0029.
Values may be sent and summed in bfloat16 or wider, within the bound.
A program may use at most 128 MiB of HBM per device.

v0:
```python
import jax
import jax.numpy as jnp
from jax import lax
from jax.sharding import PartitionSpec as P

BLK = 256
MAXDEPTH = 4


def from_behind(block, axis, distance):
    devices = range(lax.axis_size(axis))
    route = [(i - distance, i) for i in devices if i - distance in devices]
    return lax.ppermute(block, axis, route)


def body(dosage, effects, depth):
    block = BLK
    span = MAXDEPTH + 1
    local_blocks = depth.shape[0]
    samples_all = dosage.shape[0] * lax.axis_size("samp")
    following = from_behind((dosage, effects), "genome", -1)
    window_x = jnp.concatenate([dosage, following[0]], axis=1)
    window_b = jnp.concatenate([effects, following[1]], axis=0)
    grams = []
    for local in range(local_blocks):
        own_x = dosage[:, local * block : (local + 1) * block]
        row = []
        for offset in range(span):
            other = window_x[:, (local + offset) * block : (local + offset + 1) * block]

            def compute(own_x=own_x, other=other):
                return lax.dot_general(
                    own_x, other, (((0,), (0,)), ((), ())), preferred_element_type=jnp.float32
                )

            def skipped():
                return jnp.zeros((block, block), jnp.float32)

            if offset == 0:
                row.append(compute())
            else:
                row.append(lax.cond(offset <= depth[local], compute, skipped))
        grams.append(jnp.concatenate(row, axis=1))
    partial_grams = jnp.stack(grams, axis=0)
    summed = lax.psum(partial_grams, "samp")
    corr = (summed / jnp.float32(samples_all)).astype(jnp.bfloat16)
    traits_dev = effects.shape[1]
    results = []
    backward = jnp.zeros((local_blocks * 2, block, traits_dev), jnp.float32)
    for local in range(local_blocks):
        window = window_b[local * block : (local + span) * block]
        results.append(jnp.dot(corr[local], window, preferred_element_type=jnp.float32))
        own_b = effects[local * block : (local + 1) * block]
        transposed = lax.dot_general(
            corr[local][:, block:],
            own_b,
            (((0,), (0,)), ((), ())),
            preferred_element_type=jnp.float32,
        )
        transposed = transposed.reshape(MAXDEPTH, block, traits_dev)
        backward = backward.at[local + 1 : local + span].add(transposed)
    received = from_behind(backward[local_blocks:], "genome", 1)
    total = jnp.stack(results, axis=0) + backward[:local_blocks] + received
    return total.reshape(local_blocks * block, traits_dev)


def solution(mesh):
    return jax.shard_map(
        body,
        mesh=mesh,
        in_specs=(P("samp", "genome"), P("genome", "samp"), P("genome")),
        out_specs=P("genome", "samp"),
        check_vma=False,
    )
```

profile of v0, /device:TPU:0, one launch (start us, length us, event | category | flops | bytes accessed | tf_op | source)
XLA Modules:
  0.0 355.1 jit_solution(9601656168017734934)
XLA Ops:
  15.0 5.4 %fusion.24 = (bf16[4096,256]{1,0:T(8,128)(2,1)S(1)}, bf16[4096,256]{1,0:T(8,128)(2,1)S(1)}, bf16[4096,256]{1,0:T(8,128)(2,1)}, bf16[4096,256]{1,0:T(8,128)(2,1)}) fusion(bf16[4096,1024]{1,0:T(8,128)(2,1)} %param.43), kind=kLoop, calls=%fused_computation.60 | loop fusion | bytes 16777216 | tf_op jit(solution)/shard_map/slice | solution.py:26
  26.7 3.2 conditional.20
  26.8 3.1 fusion.31
  29.9 3.2 conditional.21
  29.9 3.1 fusion.32
  33.1 2.5 conditional.16
  36.4 3.2 convolution_dynamic-update-slice_fusion.1
  39.7 3.6 %convolution_dynamic-update-slice_fusion.2 = f32[256,1280]{0,1:T(8,128)S(1)} fusion(bf16[4096,1024]{1,0:T(8,128)(2,1)} %param.43), kind=kOutput, calls=%fused_computation.6 | convolution fusion | flops 536870912 | bytes 2359296 | tf_op jit(solution)/shard_map/dot_general | solution.py:32
  43.4 3.6 %convolution_dynamic-update-slice_fusion.3 = f32[256,1280]{0,1:T(8,128)S(1)} fusion(bf16[4096,1024]{1,0:T(8,128)(2,1)} %param.43), kind=kOutput, calls=%fused_computation.7 | convolution fusion | flops 536870912 | bytes 2359296 | tf_op jit(solution)/shard_map/dot_general | solution.py:32
  48.1 3.6 %convolution_dynamic-update-slice_fusion = f32[256,1280]{0,1:T(8,128)S(1)} fusion(bf16[4096,1024]{1,0:T(8,128)(2,1)} %param.43), kind=kOutput, calls=%fused_computation.4 | convolution fusion | flops 536870912 | bytes 2359296 | tf_op jit(solution)/shard_map/dot_general | solution.py:32
  51.7 140.4 %collective-permute-done = bf16[4096,1024]{1,0:T(8,128)(2,1)} collective-permute-done((bf16[4096,1024]{1,0:T(8,128)(2,1)}, bf16[4096,1024]{1,0:T(8,128)(2,1)}, u32[]{:S(2)}, u32[]{:S(2)}) %collective-permute-start) | collective-permute-done | bytes 8388640 | tf_op jit(solution)/shard_map/ppermute | solution.py:13
  192.1 5.3 %fusion.25 = (bf16[4096,256]{1,0:T(8,128)(2,1)}, bf16[4096,256]{1,0:T(8,128)(2,1)}, bf16[4096,256]{1,0:T(8,128)(2,1)S(1)}) fusion(bf16[4096,1024]{1,0:T(8,128)(2,1)} %collective-permute-done), kind=kLoop, calls=%fused_computation.61 | loop fusion | bytes 12582912 | tf_op jit(solution)/shard_map/slice | solution.py:29
  200.0 3.2 conditional.29
  200.0 3.1 fusion.40
  206.8 3.1 conditional.26
  206.8 3.1 fusion.37
  210.7 3.1 conditional.27
  210.7 3.1 fusion.38
  216.9 4.8 %pad_maximum_fusion = f32[4,256,1280]{1,2,0:T(8,128)} fusion(f32[1,256,1280]{1,2,0:T(8,128)S(1)} %bitcast.80, f32[1,256,1280]{1,2,0:T(8,128)} %bitcast.81, f32[1,256,1280]{1,2,0:T(8,128)} %bitcast.82, f32[1,256,1280]{1,2,0:T(8,128)} %bitcast.83), kind=kLoop, calls=%fused_computation.2 | loop fusion | flops 3932160 | bytes 10485760 | tf_op jit(solution)/shard_map/stack | solution.py:44
  223.9 8.1 %collective-permute-done.1 = bf16[1024,128]{1,0:T(8,128)(2,1)S(1)} collective-permute-done((bf16[1024,128]{1,0:T(8,128)(2,1)S(1)}, bf16[1024,128]{1,0:T(8,128)(2,1)S(1)}, u32[]{:S(2)}, u32[]{:S(2)}) %collective-permute-start.1) | collective-permute-done | bytes 262176 | tf_op jit(solution)/shard_map/ppermute | solution.py:13
  232.0 96.2 %all-reduce.3.cloned.1.call-done = f32[4,256,1280]{1,2,0:T(8,128)} async-done(((f32[4,256,1280]{1,2,0:T(8,128)}), f32[4,256,1280]{1,2,0:T(8,128)}) %all-reduce.3.cloned.1.call-update) | async-done | bytes 5242896 | tf_op jit(solution)/shard_map/psum | solution.py:45
  328.2 3.0 multiply_convert_fusion
  333.0 3.4 collective-permute-start.2
  337.9 9.5 %collective-permute-done.2 = f32[4,256,128]{2,1,0:T(8,128)S(1)} collective-permute-done((f32[4,256,128]{2,1,0:T(8,128)S(1)}, f32[4,256,128]{2,1,0:T(8,128)S(1)}, u32[]{:S(2)}, u32[]{:S(2)}) %collective-permute-start.2) | collective-permute-done | bytes 524320 | tf_op jit(solution)/shard_map/ppermute | solution.py:13
  (70 shorter events, 34.2 us)
Async XLA Ops:
  6.5 321.7 %all-reduce.3.cloned.1.call-start = ((), (), s32[]{:S(2)}) async-start(), calls=%async_computation | async-start | bytes 10485760 | tf_op jit(solution)/shard_map/psum | solution.py:45
  6.5 185.6 %collective-permute-start = (bf16[4096,1024]{1,0:T(8,128)(2,1)}, bf16[4096,1024]{1,0:T(8,128)(2,1)}, u32[]{:S(2)}, u32[]{:S(2)}) collective-permute-start(bf16[4096,1024]{1,0:T(8,128)(2,1)} %param.43), channel_id=1, source_target_pairs={{4,0},{8,4},{12,8},{16,12},{20,16},{24,20},{28,24},{5,1},{9,5},{13... | collective-permute-start | bytes 25165832 | tf_op jit(solution)/shard_map/ppermute | solution.py:13
  20.4 3.8 %copy-start.1 = (bf16[4096,256]{1,0:T(8,128)(2,1)}, bf16[4096,256]{1,0:T(8,128)(2,1)S(1)}, u32[]{:S(2)}) copy-start(bf16[4096,256]{1,0:T(8,128)(2,1)S(1)} %get-tuple-element.215) | copy-start | bytes 6291460
  20.4 15.3 %copy-start = (bf16[4096,256]{1,0:T(8,128)(2,1)}, bf16[4096,256]{1,0:T(8,128)(2,1)S(1)}, u32[]{:S(2)}) copy-start(bf16[4096,256]{1,0:T(8,128)(2,1)S(1)} %get-tuple-element.214) | copy-start | bytes 6291460
  39.6 3.7 %copy-start.2 = (f32[256,1280]{0,1:T(8,128)}, f32[256,1280]{0,1:T(8,128)S(1)}, u32[]{:S(2)}) copy-start(f32[256,1280]{0,1:T(8,128)S(1)} %constant_dynamic-update-slice_fusion.11) | copy-start | bytes 3932164
  43.4 3.7 %copy-start.3 = (f32[256,1280]{0,1:T(8,128)}, f32[256,1280]{0,1:T(8,128)S(1)}, u32[]{:S(2)}) copy-start(f32[256,1280]{0,1:T(8,128)S(1)} %constant_dynamic-update-slice_fusion.6) | copy-start | bytes 3932164
  48.1 3.7 %copy-start.4 = (f32[256,1280]{0,1:T(8,128)}, f32[256,1280]{0,1:T(8,128)S(1)}, u32[]{:S(2)}) copy-start(f32[256,1280]{0,1:T(8,128)S(1)} %constant_dynamic-update-slice_fusion.1) | copy-start | bytes 3932164
  221.6 0.9 copy-start.5
  222.6 9.4 %collective-permute-start.1 = (bf16[1024,128]{1,0:T(8,128)(2,1)S(1)}, bf16[1024,128]{1,0:T(8,128)(2,1)S(1)}, u32[]{:S(2)}, u32[]{:S(2)}) collective-permute-start(bf16[1024,128]{1,0:T(8,128)(2,1)S(1)} %copy-done.5), channel_id=1, source_target_pairs={{4,0},{8,4},{12,8},{16,12},{20,16},{24,20},{28,24},{5,1},{9,5},{13... | collective-permute-start | bytes 786440 | tf_op jit(solution)/shard_map/ppermute | solution.py:13
  333.0 14.4 %collective-permute-start.2 = (f32[4,256,128]{2,1,0:T(8,128)S(1)}, f32[4,256,128]{2,1,0:T(8,128)S(1)}, u32[]{:S(2)}, u32[]{:S(2)}) collective-permute-start(f32[4,256,128]{2,1,0:T(8,128)S(1)} %slice_add_fusion), channel_id=1, source_target_pairs={{0,4},{4,8},{8,12},{12,16},{16,20},{20,24},{24,28},{1,5},{5,9},{9,... | collective-permute-start | bytes 1572872 | tf_op jit(solution)/shard_map/ppermute | solution.py:13
Sparse Core Ops, SparseCore 0:
  221.8 106.4 all-reduce.2
where the time goes:
time: 357 us; the launch traced here: 355 us
  waiting for transfers between devices  254 us (71%)
  matrix products  42.6 us (12%)
  between operations  23.3 us (7%)
  local copies, waits for them, and re-layouts  19.7 us (6%)
  other arithmetic  8.87 us (2%)
  starting transfers between devices  5.95 us (2%)
    ppermute x3, waiting for transfers between devices, from_behind(): return lax.ppermute(block, axis, route)  158 us
    psum x1, waiting for transfers between devices, body(): summed = lax.psum(partial_grams, 'samp')  96.2 us
    cond x9, matrix products, body(): row.append(lax.cond(offset <= depth[local], compute, skipped))  25.8 us
    dot_general x4, matrix products, compute(): lax.dot_general(own_x, other, (((0,), (0,)), ((), ())), preferred_element...  14.1 us
  transfers between devices with their start and end apart: 4, of which 4 were waited for; matrix products, arithmetic and copies ran while one was open for 10% of the time, Pallas kernels for 0%

commit v1 on v0

v1 whole, which is shorter than its diff:
```python
import functools

import jax
import jax.numpy as jnp
from jax import lax
from jax.experimental import pallas as pl
from jax.experimental.pallas import tpu as pltpu
from jax.sharding import PartitionSpec as P

BLK = 256
MESH = pl.DeviceIdType.MESH
F32 = jnp.float32
BF16 = jnp.bfloat16
CONTRACT0 = (((0,), (0,)), ((), ()))


def gram(left, right):
    return lax.dot_general(left, right, CONTRACT0, preferred_element_type=F32)


def kernel(
    n_genome, n_samp, nb, half, traits, scale,
    x_ref, e_ref, d_ref, out_ref,
    own, xbuf, zbuf, eff, dep, loc, cro, par, far, stage, rs_loc, rs, hop_out, hop_in,
    own_sem, own_e_sem, x_send, x_recv, z_send, z_recv, es_send, es_recv, ex_send, ex_recv,
    ds_send, ds_recv, ef_send, ef_recv, rl_send, rl_recv, rs_send, rs_recv, h_send, h_recv,
):
    g = lax.axis_index("genome")
    s = lax.axis_index("samp")
    q = lax.rem(g, 2)
    sign = 1 - 2 * q
    partner = g + sign
    z_from = g + 2 * sign
    z_to = g - 2 * sign
    has_from = jnp.logical_and(z_from >= 0, z_from < n_genome)
    has_to = jnp.logical_and(z_to >= 0, z_to < n_genome)

    def mine(u):
        return u + q * (nb - 1 - 2 * u)

    def other(u):
        return nb - 1 - mine(u)

    def peer(d):
        return lax.rem(s + d, n_samp)

    def cols(t):
        return pl.ds(pl.multiple_of(t * traits, traits), traits)

    my_cols = cols(s)
    keep_rows = pl.ds(pl.multiple_of(q * half, half), half)
    give_rows = pl.ds(pl.multiple_of((1 - q) * half, half), half)

    def remote(src, dst, ss, rsem, gg, sss):
        return pltpu.make_async_remote_copy(
            src_ref=src, dst_ref=dst, send_sem=ss, recv_sem=rsem,
            device_id=(gg, sss), device_id_type=MESH,
        )

    barrier = pltpu.get_barrier_semaphore()
    for d in range(1, n_samp):
        pl.semaphore_signal(barrier, inc=1, device_id=(g, peer(d)), device_id_type=MESH)
    pl.semaphore_signal(barrier, inc=1, device_id=(partner, s), device_id_type=MESH)

    @pl.when(has_from)
    def _():
        pl.semaphore_signal(barrier, inc=1, device_id=(z_from, s), device_id_type=MESH)

    @pl.when(has_to)
    def _():
        pl.semaphore_signal(barrier, inc=1, device_id=(z_to, s), device_id_type=MESH)

    own_copies = [
        pltpu.make_async_copy(x_ref.at[:, b * BLK : (b + 1) * BLK], own.at[b], own_sem.at[b])
        for b in range(nb)
    ]
    own_e = pltpu.make_async_copy(e_ref, eff.at[0, :, my_cols], own_e_sem.at[0])
    own_e.start()
    for c in own_copies:
        c.start()
    pl.semaphore_wait(
        barrier, n_samp + has_from.astype(jnp.int32) + has_to.astype(jnp.int32)
    )

    def block_cols(b):
        return pl.ds(pl.multiple_of(b * BLK, BLK), BLK)

    x_copies = [
        remote(x_ref.at[give_rows, block_cols(other(t))], xbuf.at[t], x_send.at[t], x_recv.at[t], partner, s)
        for t in range(nb)
    ]
    z_copies = [
        remote(x_ref.at[keep_rows, block_cols(mine(t))], zbuf.at[t], z_send.at[t], z_recv.at[t], z_to, s)
        for t in range(nb)
    ]
    d_x = remote(d_ref, dep.at[0], ds_send.at[0], ds_recv.at[0], partner, s)
    d_z = remote(d_ref, dep.at[1], ds_send.at[1], ds_recv.at[1], z_to, s)
    e_x = remote(e_ref, eff.at[1, :, my_cols], ex_send.at[0], ex_recv.at[0], partner, s)
    e_z = remote(e_ref, eff.at[2, :, my_cols], ex_send.at[1], ex_recv.at[1], z_to, s)
    d_x.start()
    e_x.start()
    x_copies[0].start()
    x_copies[1].start()

    @pl.when(has_to)
    def _():
        d_z.start()
        e_z.start()
        z_copies[0].start()
        z_copies[1].start()

    e_s = [
        remote(e_ref, eff.at[0, :, my_cols], es_send.at[d - 1], es_recv.at[d - 1], g, peer(d))
        for d in range(1, n_samp)
    ]
    for c in e_s:
        c.start()

    loc[...] = jnp.zeros_like(loc)
    cro[...] = jnp.zeros_like(cro)
    par[...] = jnp.zeros_like(par)
    far[...] = jnp.zeros_like(far)
    own_e.wait()
    for c in own_copies:
        c.wait()
    for c in e_s:
        c.wait()
    e_x.wait_recv()
    f_x = [
        remote(eff.at[1, :, my_cols], eff.at[1, :, my_cols], ef_send.at[d - 1], ef_recv.at[d - 1], g, peer(d))
        for d in range(1, n_samp)
    ]
    for c in f_x:
        c.start()
    f_z = [
        remote(
            eff.at[2, :, my_cols], eff.at[2, :, my_cols],
            ef_send.at[n_samp + d - 2], ef_recv.at[n_samp + d - 2], g, peer(d),
        )
        for d in range(1, n_samp)
    ]

    @pl.when(has_from)
    def _():
        e_z.wait_recv()
        for c in f_z:
            c.start()

    def rows(b):
        return pl.ds(pl.multiple_of(b * BLK, BLK), BLK)

    def weight(drow, k):
        return jnp.where(drow >= k.astype(F32), F32(scale), F32(0.0))

    def local_row(i, carry):
        def local_pair(j, carry):
            full = gram(own[i, :half], own[j, :half]) + gram(own[i, half:], own[j, half:])
            full = full * weight(d_ref[pl.ds(i, 1), :], j - i)
            high = full.astype(BF16)
            low = (full - high.astype(F32)).astype(BF16)
            ej = eff[0, rows(j), :]
            loc[rows(i), :] += jnp.dot(high, ej, preferred_element_type=F32) + jnp.dot(
                low, ej, preferred_element_type=F32
            )

            @pl.when(j > i)
            def _():
                ei = eff[0, rows(i), :]
                loc[rows(j), :] += gram(high, ei) + gram(low, ei)

            return carry

        return lax.fori_loop(i, nb, local_pair, carry)

    lax.fori_loop(0, nb, local_row, 0)
    rl = [
        remote(loc.at[:, cols(peer(d))], rs_loc.at[d - 1], rl_send.at[d - 1], rl_recv.at[d - 1], g, peer(d))
        for d in range(1, n_samp)
    ]
    for c in rl:
        c.start()

    for c in f_x:
        c.wait_recv()
    d_x.wait_recv()

    @pl.when(has_from)
    def _():
        for c in f_z:
            c.wait_recv()
        d_z.wait_recv()

    kinds = {"own": (0, cro), "partner": (1, par), "far": (2, far)}

    def scatter(kind, t):
        n, _ = kinds[kind]
        return [
            remote(
                stage.at[n, t, :, cols(peer(d))], rs.at[n, t, d - 1],
                rs_send.at[n, t, d - 1], rs_recv.at[n, t, d - 1], g, peer(d),
            )
            for d in range(1, n_samp)
        ]

    def publish(kind, t):
        n, acc = kinds[kind]
        stage[n, t] = acc[t * BLK : (t + 1) * BLK, :].astype(BF16)
        for c in scatter(kind, t):
            c.start()

    def collect(kind, t):
        n, acc = kinds[kind]
        for c in scatter(kind, t):
            c.wait_recv()
        total = acc[t * BLK : (t + 1) * BLK, my_cols]
        for d in range(1, n_samp):
            total = total + rs[n, t, d - 1].astype(F32)
        return total

    def hop(n, t):
        return remote(
            hop_out.at[n, t], hop_in.at[n, t], h_send.at[n, t], h_recv.at[n, t],
            partner if n == 0 else z_from, s,
        )

    def forward(n, t):
        hop_out[n, t] = collect("partner" if n == 0 else "far", t).astype(BF16)
        hop(n, t).start()

    for t in range(nb):
        x_copies[t].wait_recv()
        if t + 2 < nb:
            x_copies[t].wait_send()
            x_copies[t + 2].start()

            @pl.when(has_to)
            def _():
                z_copies[t].wait_send()
                z_copies[t + 2].start()

        def x_pair(u, carry):
            k = nb + t - u
            mu, mt = mine(u), mine(t)
            drow = jnp.where(q == 0, d_ref[pl.ds(mu, 1), :], dep[0, pl.ds(mt, 1), :])
            full = gram(own[mu, keep_rows, :], xbuf[t]) * weight(drow, k)
            high = full.astype(BF16)
            cro[rows(u), :] += jnp.dot(high, eff[1, rows(other(nb - 1 - t)), :], preferred_element_type=F32)
            par[t * BLK : (t + 1) * BLK, :] += gram(high, eff[0, rows(mu), :])
            return carry

        lax.fori_loop(t, nb, x_pair, 0)
        publish("own", t)

        @pl.when(has_from)
        def _():
            z_copies[t].wait_recv()

            def z_pair(v, carry):
                k = nb + v - t
                mt, mv = mine(t), mine(v)
                drow = jnp.where(q == 0, dep[0, pl.ds(mt, 1), :], dep[1, pl.ds(mv, 1), :])
                full = gram(xbuf[t], zbuf[v]) * weight(drow, jnp.int32(0) + k)
                high = full.astype(BF16)
                par[t * BLK : (t + 1) * BLK, :] += jnp.dot(high, eff[2, rows(mv), :], preferred_element_type=F32)
                far[rows(v), :] += gram(high, eff[1, rows(mt), :])
                return carry

            lax.fori_loop(0, t + 1, z_pair, 0)

        publish("partner", t)
        if t > 0:
            forward(0, t - 1)

    @pl.when(has_from)
    def _():
        for v in range(nb):
            publish("far", v)
    forward(0, nb - 1)

    for c in rl:
        c.wait_recv()
    total = loc[:, my_cols]
    for d in range(1, n_samp):
        total = total + rs_loc[d - 1]
    out_ref[...] = total
    for t in range(nb):
        part = collect("own", t)
        out_ref[rows(mine(t)), :] += part

    @pl.when(has_from)
    def _():
        for v in range(nb):
            forward(1, v)
    for t in range(nb):
        hop(0, t).wait_recv()
        out_ref[rows(other(t)), :] += hop_in[0, t].astype(F32)

    @pl.when(has_to)
    def _():
        for v in range(nb):
            hop(1, v).wait_recv()
            out_ref[rows(mine(v)), :] += hop_in[1, v].astype(F32)

    d_x.wait_send()
    e_x.wait_send()
    for t in range(nb - 2, nb):
        x_copies[t].wait_send()

    @pl.when(has_to)
    def _():
        d_z.wait_send()
        e_z.wait_send()
        for t in range(nb - 2, nb):
            z_copies[t].wait_send()

    for c in f_x + rl:
        c.wait_send()
    for t in range(nb):
        for c in scatter("own", t) + scatter("partner", t):
            c.wait_send()
        hop(0, t).wait_send()

    @pl.when(has_from)
    def _():
        for c in f_z:
            c.wait_send()
        for t in range(nb):
            for c in scatter("far", t):
                c.wait_send()
            hop(1, t).wait_send()


def body(n_genome, n_samp, dosage, effects, depth):
    nb = depth.shape[0]
    samples, variants = dosage.shape
    traits = effects.shape[1]
    all_traits = traits * n_samp
    half = samples // 2
    d = jnp.zeros((8, BLK), F32).at[:nb].set(jnp.broadcast_to(depth.astype(F32)[:, None], (nb, BLK)))
    dma = pltpu.SemaphoreType.DMA
    p = n_samp - 1
    return pl.pallas_call(
        functools.partial(kernel, n_genome, n_samp, nb, half, traits, 1.0 / (samples * n_samp)),
        out_shape=jax.ShapeDtypeStruct((variants, traits), F32),
        in_specs=[
            pl.BlockSpec(memory_space=pl.ANY),
            pl.BlockSpec(memory_space=pl.ANY),
            pl.BlockSpec(memory_space=pltpu.VMEM),
        ],
        out_specs=pl.BlockSpec(memory_space=pltpu.VMEM),
        scratch_shapes=[
            pltpu.VMEM((nb, samples, BLK), BF16),
            pltpu.VMEM((nb, half, BLK), BF16),
            pltpu.VMEM((nb, half, BLK), BF16),
            pltpu.VMEM((3, variants, all_traits), BF16),
            pltpu.VMEM((2, 8, BLK), F32),
            pltpu.VMEM((variants, all_traits), F32),
            pltpu.VMEM((variants, all_traits), F32),
            pltpu.VMEM((variants, all_traits), F32),
            pltpu.VMEM((variants, all_traits), F32),
            pltpu.VMEM((3, nb, BLK, all_traits), BF16),
            pltpu.VMEM((p, variants, traits), F32),
            pltpu.VMEM((3, nb, p, BLK, traits), BF16),
            pltpu.VMEM((2, nb, BLK, traits), BF16),
            pltpu.VMEM((2, nb, BLK, traits), BF16),
            dma((nb,)), dma((1,)),
            dma((nb,)), dma((nb,)), dma((nb,)), dma((nb,)),
            dma((p,)), dma((p,)),
            dma((2,)), dma((2,)), dma((2,)), dma((2,)),
            dma((2 * p,)), dma((2 * p,)),
            dma((p,)), dma((p,)),
            dma((3, nb, p)), dma((3, nb, p)),
            dma((2, nb)), dma((2, nb)),
        ],
        compiler_params=pltpu.CompilerParams(
            collective_id=0, has_side_effects=True, vmem_limit_bytes=60 * 1024 * 1024
        ),
        cost_estimate=pl.CostEstimate(
            flops=2 * 20 * BLK * BLK * samples, bytes_accessed=4 * samples * variants, transcendentals=0
        ),
    )(dosage, effects, d)


def solution(mesh):
    return jax.shard_map(
        functools.partial(body, mesh.shape["genome"], mesh.shape["samp"]),
        mesh=mesh,
        in_specs=(P("samp", "genome"), P("genome", "samp"), P("genome")),
        out_specs=P("genome", "samp"),
        check_vma=False,
    )
```

time: 357 us -> 129 us (0.36)
  waiting for transfers between devices: 254 us -> 0 us
  Pallas kernels: 0 us -> 126 us
  matrix products: 42.6 us -> 0 us
  between operations: 23.3 us -> 0.01 us
  local copies, waits for them, and re-layouts: 19.7 us -> 2.54 us
  other arithmetic: 8.87 us -> 0.66 us
  starting transfers between devices: 5.95 us -> 0 us
    ppermute x3 -> x0, waiting for transfers between devices: 158 us -> none  [from_behind(): return lax.ppermute(block, axis, route)]
    pallas_call x0 -> x1, Pallas kernels: none -> 126 us  [body(): pl.pallas_call(functools.partial(kernel, n_genome, n_samp, nb, half, trai...]
    psum x1 -> x0, waiting for transfers between devices: 96.2 us -> none  [body(): summed = lax.psum(partial_grams, 'samp')]
    cond x9 -> x0, matrix products: 25.8 us -> none  [body(): row.append(lax.cond(offset <= depth[local], compute, skipped))]
    dot_general x12 -> x0, matrix products: 16.8 us -> none  [the longest x4 14.1 us: compute(): lax.dot_general(own_x, other, (((0,), (0,)), ((), ())), preferred_element...]
    slice x3 -> x0, local copies, waits for them, and re-layouts: 12.1 us -> none  [the longest x1 5.43 us: body(): own_x = dosage[:, local * block:(local + 1) * block]]
    ppermute x3 -> x0, starting transfers between devices: 5.94 us -> none  [from_behind(): return lax.ppermute(block, axis, route)]
    another operation x1 -> x0, other arithmetic: 4.77 us -> none  [body(): partial_grams = jnp.stack(grams, axis=0)]
  transfers between devices with their start and end apart: 4 -> 0, of which waited for: 4 -> 0; matrix products, arithmetic and copies ran while one was open for 10% -> 0% of each run, Pallas kernels for 0% -> 0%
where the time goes in v1:
time: 129 us
  Pallas kernels  126 us (98%)
  local copies, waits for them, and re-layouts  2.54 us (2%)
    pallas_call x1, Pallas kernels, body(): pl.pallas_call(functools.partial(kernel, n_genome, n_samp, nb, half, trai...  126 us

profile of v1, /device:TPU:0, one launch (start us, length us, event | category | flops | bytes accessed | tf_op | source)
XLA Modules:
  0.0 128.8 jit_solution(12477423786574546223)
XLA Ops:
  0.0 0.7 convert_element_type.3
  0.7 0.7 scatter.8.d_ref
  1.3 125.6 %shard_map.37 = f32[1024,128]{1,0:T(8,128)} custom-call(bf16[4096,1024]{1,0:T(8,128)(2,1)} %x_ref.1, bf16[1024,128]{1,0:T(8,128)(2,1)} %e_ref.1, f32[8,256]{1,0:T(8,128)} %scatter.8.d_ref), custom_call_target="tpu_custom_call" | custom-call | flops 10737418240 | bytes 16777216 | tf_op jit(solution)/shard_map/pallas_call | solution.py:342
  126.9 1.9 %copy.5 = f32[1024,128]{1,0:T(8,128)} copy(f32[1024,128]{1,0:T(8,128)} %shard_map.37) | data formatting | bytes 1048576
  (1 shorter events, 0.0 us)

commit v2 on v1

--- a/solution.py
+++ b/solution.py
@@ -21,9 +21,9 @@
 def kernel(
     n_genome, n_samp, nb, half, traits, scale,
     x_ref, e_ref, d_ref, out_ref,
-    own, xbuf, zbuf, eff, dep, loc, cro, par, far, stage, rs_loc, rs, hop_out, hop_in,
+    own, xbuf, zbuf, eff, dep, loc, cro, par, far, lc_in, ly_out, ly_in, c_in, y_out, y_in, hop_out, hop_in,
     own_sem, own_e_sem, x_send, x_recv, z_send, z_recv, es_send, es_recv, ex_send, ex_recv,
-    ds_send, ds_recv, ef_send, ef_recv, rl_send, rl_recv, rs_send, rs_recv, h_send, h_recv,
+    ds_send, ds_recv, lc_send, lc_recv, ly_send, ly_recv, c_send, c_recv, y_send, y_recv, h_send, h_recv,
 ):
     g = lax.axis_index("genome")
     s = lax.axis_index("samp")
@@ -41,8 +41,9 @@
     def other(u):
         return nb - 1 - mine(u)
 
-    def peer(d):
-        return lax.rem(s + d, n_samp)
+    core = lax.rem(s, 2)
+    core_mate = s + 1 - 2 * core
+    cross_mate = lax.rem(s + 2, n_samp)
 
     def cols(t):
         return pl.ds(pl.multiple_of(t * traits, traits), traits)
@@ -58,8 +59,8 @@
         )
 
     barrier = pltpu.get_barrier_semaphore()
-    for d in range(1, n_samp):
-        pl.semaphore_signal(barrier, inc=1, device_id=(g, peer(d)), device_id_type=MESH)
+    for mate in (core_mate, cross_mate):
+        pl.semaphore_signal(barrier, inc=1, device_id=(g, mate), device_id_type=MESH)
     pl.semaphore_signal(barrier, inc=1, device_id=(partner, s), device_id_type=MESH)
 
     @pl.when(has_from)
@@ -79,7 +80,7 @@
     for c in own_copies:
         c.start()
     pl.semaphore_wait(
-        barrier, n_samp + has_from.astype(jnp.int32) + has_to.astype(jnp.int32)
+        barrier, 3 + has_from.astype(jnp.int32) + has_to.astype(jnp.int32)
     )
 
     def block_cols(b):
@@ -109,48 +110,48 @@
         z_copies[0].start()
         z_copies[1].start()
 
-    e_s = [
-        remote(e_ref, eff.at[0, :, my_cols], es_send.at[d - 1], es_recv.at[d - 1], g, peer(d))
-        for d in range(1, n_samp)
-    ]
-    for c in e_s:
-        c.start()
-
+    def gather(slot, source):
+        across = cols(cross_mate)
+        here = eff.at[slot, :, my_cols]
+        there = eff.at[slot, :, across]
+        return [
+            remote(source, here, es_send.at[slot, 0], es_recv.at[slot, 0], g, core_mate),
+            remote(source, here, es_send.at[slot, 1], es_recv.at[slot, 1], g, cross_mate),
+            remote(there, there, es_send.at[slot, 2], es_recv.at[slot, 2], g, core_mate),
+        ]
+
+    e_own = gather(0, e_ref)
+    e_partner = gather(1, eff.at[1, :, my_cols])
+    e_far = gather(2, eff.at[2, :, my_cols])
+    e_own[0].start()
+    e_own[1].start()
     loc[...] = jnp.zeros_like(loc)
     cro[...] = jnp.zeros_like(cro)
     par[...] = jnp.zeros_like(par)
     far[...] = jnp.zeros_like(far)
+    e_own[1].wait_recv()
+    e_own[2].start()
+    e_x.wait_recv()
+    e_partner[0].start()
+    e_partner[1].start()
+
+    @pl.when(has_from)
+    def _():
+        e_z.wait_recv()
+        e_far[0].start()
+        e_far[1].start()
+
     own_e.wait()
     for c in own_copies:
         c.wait()
-    for c in e_s:
-        c.wait()
-    e_x.wait_recv()
-    f_x = [
-        remote(eff.at[1, :, my_cols], eff.at[1, :, my_cols], ef_send.at[d - 1], ef_recv.at[d - 1], g, peer(d))
-        for d in range(1, n_samp)
-    ]
-    for c in f_x:
-        c.start()
-    f_z = [
-        remote(
-            eff.at[2, :, my_cols], eff.at[2, :, my_cols],
-            ef_send.at[n_samp + d - 2], ef_recv.at[n_samp + d - 2], g, peer(d),
-        )
-        for d in range(1, n_samp)
-    ]
-
-    @pl.when(has_from)
-    def _():
-        e_z.wait_recv()
-        for c in f_z:
-            c.start()
+    e_own[0].wait_recv()
+    e_own[2].wait_recv()
+
+    def weight(drow, k):
+        return jnp.where(drow >= k.astype(F32), F32(scale), F32(0.0))
 
     def rows(b):
         return pl.ds(pl.multiple_of(b * BLK, BLK), BLK)
-
-    def weight(drow, k):
-        return jnp.where(drow >= k.astype(F32), F32(scale), F32(0.0))
 
     def local_row(i, carry):
         def local_pair(j, carry):
@@ -173,49 +174,72 @@
         return lax.fori_loop(i, nb, local_pair, carry)
 
     lax.fori_loop(0, nb, local_row, 0)
-    rl = [
-        remote(loc.at[:, cols(peer(d))], rs_loc.at[d - 1], rl_send.at[d - 1], rl_recv.at[d - 1], g, peer(d))
-        for d in range(1, n_samp)
-    ]
-    for c in rl:
-        c.start()
-
-    for c in f_x:
-        c.wait_recv()
+    def loc_core(y):
+        return remote(
+            loc.at[:, cols(2 * y + 1 - core)], lc_in.at[y], lc_send.at[y], lc_recv.at[y], g, core_mate
+        )
+
+    loc_across = remote(ly_out, ly_in, ly_send.at[0], ly_recv.at[0], g, cross_mate)
+    loc_core(0).start()
+    loc_core(1).start()
+    e_partner[1].wait_recv()
+    e_partner[2].start()
     d_x.wait_recv()
 
     @pl.when(has_from)
     def _():
-        for c in f_z:
-            c.wait_recv()
+        e_far[1].wait_recv()
+        e_far[2].start()
         d_z.wait_recv()
 
+    my_y = s // 2
+    mate_y = 1 - my_y
+    loc_core(0).wait_recv()
+    loc_core(1).wait_recv()
+    ly_out[...] = loc[:, cols(cross_mate)] + lc_in[mate_y]
+    loc_across.start()
+    e_partner[0].wait_recv()
+    e_partner[2].wait_recv()
+
+    @pl.when(has_from)
+    def _():
+        e_far[0].wait_recv()
+        e_far[2].wait_recv()
+
     kinds = {"own": (0, cro), "partner": (1, par), "far": (2, far)}
 
-    def scatter(kind, t):
-        n, _ = kinds[kind]
+    def block_rows(t):
+        return pl.ds(t * BLK, BLK)
+
+    def to_core(kind, t):
+        n, acc = kinds[kind]
         return [
             remote(
-                stage.at[n, t, :, cols(peer(d))], rs.at[n, t, d - 1],
-                rs_send.at[n, t, d - 1], rs_recv.at[n, t, d - 1], g, peer(d),
+                acc.at[block_rows(t), cols(2 * y + 1 - core)], c_in.at[n, t, y],
+                c_send.at[n, t, y], c_recv.at[n, t, y], g, core_mate,
             )
-            for d in range(1, n_samp)
+            for y in range(2)
         ]
 
+    def across(kind, t):
+        n, _ = kinds[kind]
+        return remote(y_out.at[n, t], y_in.at[n, t], y_send.at[n, t], y_recv.at[n, t], g, cross_mate)
+
     def publish(kind, t):
+        for c in to_core(kind, t):
+            c.start()
+
+    def relay(kind, t):
         n, acc = kinds[kind]
-        stage[n, t] = acc[t * BLK : (t + 1) * BLK, :].astype(BF16)
-        for c in scatter(kind, t):
-            c.start()
+        for c in to_core(kind, t):
+            c.wait_recv()
+        y_out[n, t] = (acc[block_rows(t), cols(cross_mate)] + c_in[n, t, mate_y]).astype(BF16)
+        across(kind, t).start()
 
     def collect(kind, t):
         n, acc = kinds[kind]
-        for c in scatter(kind, t):
-            c.wait_recv()
-        total = acc[t * BLK : (t + 1) * BLK, my_cols]
-        for d in range(1, n_samp):
-            total = total + rs[n, t, d - 1].astype(F32)
-        return total
+        across(kind, t).wait_recv()
+        return acc[block_rows(t), my_cols] + c_in[n, t, my_y] + y_in[n, t].astype(F32)
 
     def hop(n, t):
         return remote(
@@ -248,8 +272,9 @@
             par[t * BLK : (t + 1) * BLK, :] += gram(high, eff[0, rows(mu), :])
             return carry
 
-        lax.fori_loop(t, nb, x_pair, 0)
-        publish("own", t)
+        if t > 0:
+            relay("partner", t - 1)
+            relay("own", t - 1)
 
         @pl.when(has_from)
         def _():
@@ -265,32 +290,39 @@
                 far[rows(v), :] += gram(high, eff[1, rows(mt), :])
                 return carry
 
-            lax.fori_loop(0, t + 1, z_pair, 0)
-
+            if t < nb - 1:
+                lax.fori_loop(0, t + 1, z_pair, 0)
+            else:
+                for v in range(nb):
+                    z_pair(jnp.int32(v), 0)
+                    publish("far", v)
+
+        lax.fori_loop(t, nb, x_pair, 0)
         publish("partner", t)
+        publish("own", t)
         if t > 0:
             forward(0, t - 1)
 
     @pl.when(has_from)
     def _():
         for v in range(nb):
-            publish("far", v)
-    forward(0, nb - 1)
-
-    for c in rl:
-        c.wait_recv()
-    total = loc[:, my_cols]
-    for d in range(1, n_samp):
-        total = total + rs_loc[d - 1]
-    out_ref[...] = total
-    for t in range(nb):
-        part = collect("own", t)
-        out_ref[rows(mine(t)), :] += part
+            relay("far", v)
+
+    relay("partner", nb - 1)
+    relay("own", nb - 1)
+
+    loc_across.wait_recv()
+    out_ref[...] = loc[:, my_cols] + lc_in[my_y] + ly_in[...]
+    for t in range(nb - 1):
+        out_ref[rows(mine(t)), :] += collect("own", t)
 
     @pl.when(has_from)
     def _():
         for v in range(nb):
             forward(1, v)
+
+    forward(0, nb - 1)
+    out_ref[rows(mine(nb - 1)), :] += collect("own", nb - 1)
     for t in range(nb):
         hop(0, t).wait_recv()
         out_ref[rows(other(t)), :] += hop_in[0, t].astype(F32)
@@ -313,19 +345,20 @@
         for t in range(nb - 2, nb):
             z_copies[t].wait_send()
 
-    for c in f_x + rl:
+    for c in e_own + e_partner + [loc_core(0), loc_core(1), loc_across]:
         c.wait_send()
     for t in range(nb):
-        for c in scatter("own", t) + scatter("partner", t):
-            c.wait_send()
+        for kind in ("own", "partner"):
+            for c in to_core(kind, t) + [across(kind, t)]:
+                c.wait_send()
         hop(0, t).wait_send()
 
     @pl.when(has_from)
     def _():
-        for c in f_z:
+        for c in e_far:
             c.wait_send()
         for t in range(nb):
-            for c in scatter("far", t):
+            for c in to_core("far", t) + [across("far", t)]:
                 c.wait_send()
             hop(1, t).wait_send()
 
@@ -338,7 +371,6 @@
     half = samples // 2
     d = jnp.zeros((8, BLK), F32).at[:nb].set(jnp.broadcast_to(depth.astype(F32)[:, None], (nb, BLK)))
     dma = pltpu.SemaphoreType.DMA
-    p = n_samp - 1
     return pl.pallas_call(
         functools.partial(kernel, n_genome, n_samp, nb, half, traits, 1.0 / (samples * n_samp)),
         out_shape=jax.ShapeDtypeStruct((variants, traits), F32),
@@ -358,18 +390,20 @@
             pltpu.VMEM((variants, all_traits), F32),
             pltpu.VMEM((variants, all_traits), F32),
             pltpu.VMEM((variants, all_traits), F32),
-            pltpu.VMEM((3, nb, BLK, all_traits), BF16),
-            pltpu.VMEM((p, variants, traits), F32),
-            pltpu.VMEM((3, nb, p, BLK, traits), BF16),
+            pltpu.VMEM((2, variants, traits), F32),
+            pltpu.VMEM((variants, traits), F32),
+            pltpu.VMEM((variants, traits), F32),
+            pltpu.VMEM((3, nb, 2, BLK, traits), F32),
+            pltpu.VMEM((3, nb, BLK, traits), BF16),
+            pltpu.VMEM((3, nb, BLK, traits), BF16),
             pltpu.VMEM((2, nb, BLK, traits), BF16),
             pltpu.VMEM((2, nb, BLK, traits), BF16),
             dma((nb,)), dma((1,)),
             dma((nb,)), dma((nb,)), dma((nb,)), dma((nb,)),
-            dma((p,)), dma((p,)),
+            dma((3, 3)), dma((3, 3)),
             dma((2,)), dma((2,)), dma((2,)), dma((2,)),
-            dma((2 * p,)), dma((2 * p,)),
-            dma((p,)), dma((p,)),
-            dma((3, nb, p)), dma((3, nb, p)),
+            dma((2,)), dma((2,)), dma((1,)), dma((1,)),
+            dma((3, nb, 2)), dma((3, nb, 2)), dma((3, nb)), dma((3, nb)),
             dma((2, nb)), dma((2, nb)),
         ],
         compiler_params=pltpu.CompilerParams(

time: 129 us -> 124 us (0.961)
  Pallas kernels: 126 us -> 120 us
    pallas_call x1, Pallas kernels: 126 us -> 120 us  [body(): pl.pallas_call(functools.partial(kernel, n_genome, n_samp, nb, half, trai...]
where the time goes in v2:
time: 124 us; the launch traced here: 123 us
  Pallas kernels  120 us (97%)
  local copies, waits for them, and re-layouts  2.54 us (2%)
    pallas_call x1, Pallas kernels, body(): pl.pallas_call(functools.partial(kernel, n_genome, n_samp, nb, half, trai...  120 us

profile of v2, /device:TPU:0, one launch (start us, length us, event | category | flops | bytes accessed | tf_op | source)
XLA Modules:
  0.0 123.3 jit_solution(180109881243900855)
XLA Ops:
  0.0 0.7 convert_element_type.3
  0.7 0.7 scatter.8.d_ref
  1.3 120.1 %shard_map.37 = f32[1024,128]{1,0:T(8,128)} custom-call(bf16[4096,1024]{1,0:T(8,128)(2,1)} %x_ref.1, bf16[1024,128]{1,0:T(8,128)(2,1)} %e_ref.1, f32[8,256]{1,0:T(8,128)} %scatter.8.d_ref), custom_call_target="tpu_custom_call" | custom-call | flops 10737418240 | bytes 16777216 | tf_op jit(solution)/shard_map/pallas_call | solution.py:374
  121.4 1.9 %copy.5 = f32[1024,128]{1,0:T(8,128)} copy(f32[1024,128]{1,0:T(8,128)} %shard_map.37) | data formatting | bytes 1048576
  (1 shorter events, 0.0 us)

commit v3 on v2

--- a/solution.py
+++ b/solution.py
@@ -20,8 +20,8 @@
 
 def kernel(
     n_genome, n_samp, nb, half, traits, scale,
-    x_ref, e_ref, d_ref, out_ref,
-    own, xbuf, zbuf, eff, dep, loc, cro, par, far, lc_in, ly_out, ly_in, c_in, y_out, y_in, hop_out, hop_in,
+    x_ref, e_ref, depth_ref, out_ref,
+    d_ref, own, xbuf, zbuf, eff, dep, loc, cro, par, far, lc_in, ly_out, ly_in, c_in, y_out, y_in, hop_out, hop_in,
     own_sem, own_e_sem, x_send, x_recv, z_send, z_recv, es_send, es_recv, ex_send, ex_recv,
     ds_send, ds_recv, lc_send, lc_recv, ly_send, ly_recv, c_send, c_recv, y_send, y_recv, h_send, h_recv,
 ):
@@ -82,6 +82,9 @@
     pl.semaphore_wait(
         barrier, 3 + has_from.astype(jnp.int32) + has_to.astype(jnp.int32)
     )
+
+    for b in range(nb):
+        d_ref[b : b + 1, :] = jnp.full((1, BLK), depth_ref[b].astype(F32))
 
     def block_cols(b):
         return pl.ds(pl.multiple_of(b * BLK, BLK), BLK)
@@ -247,12 +250,18 @@
             partner if n == 0 else z_from, s,
         )
 
+    def prepare(n, t):
+        hop_out[n, t] = collect("partner" if n == 0 else "far", t).astype(BF16)
+
     def forward(n, t):
-        hop_out[n, t] = collect("partner" if n == 0 else "far", t).astype(BF16)
+        prepare(n, t)
         hop(n, t).start()
 
     for t in range(nb):
         x_copies[t].wait_recv()
+        if t == nb - 1:
+            for j in range(nb - 2):
+                hop(0, j).start()
         if t + 2 < nb:
             x_copies[t].wait_send()
             x_copies[t + 2].start()
@@ -300,14 +309,15 @@
         lax.fori_loop(t, nb, x_pair, 0)
         publish("partner", t)
         publish("own", t)
-        if t > 0:
-            forward(0, t - 1)
+        if 0 < t < nb - 1:
+            prepare(0, t - 1)
 
     @pl.when(has_from)
     def _():
         for v in range(nb):
             relay("far", v)
 
+    forward(0, nb - 2)
     relay("partner", nb - 1)
     relay("own", nb - 1)
 
@@ -369,7 +379,6 @@
     traits = effects.shape[1]
     all_traits = traits * n_samp
     half = samples // 2
-    d = jnp.zeros((8, BLK), F32).at[:nb].set(jnp.broadcast_to(depth.astype(F32)[:, None], (nb, BLK)))
     dma = pltpu.SemaphoreType.DMA
     return pl.pallas_call(
         functools.partial(kernel, n_genome, n_samp, nb, half, traits, 1.0 / (samples * n_samp)),
@@ -377,10 +386,11 @@
         in_specs=[
             pl.BlockSpec(memory_space=pl.ANY),
             pl.BlockSpec(memory_space=pl.ANY),
-            pl.BlockSpec(memory_space=pltpu.VMEM),
+            pl.BlockSpec(memory_space=pltpu.SMEM),
         ],
         out_specs=pl.BlockSpec(memory_space=pltpu.VMEM),
         scratch_shapes=[
+            pltpu.VMEM((8, BLK), F32),
             pltpu.VMEM((nb, samples, BLK), BF16),
             pltpu.VMEM((nb, half, BLK), BF16),
             pltpu.VMEM((nb, half, BLK), BF16),
@@ -412,7 +422,7 @@
         cost_estimate=pl.CostEstimate(
             flops=2 * 20 * BLK * BLK * samples, bytes_accessed=4 * samples * variants, transcendentals=0
         ),
-    )(dosage, effects, d)
+    )(dosage, effects, depth)
 
 
 def solution(mesh):

time: 124 us -> 122 us (0.984)
  no operation moved by 1% of the time
where the time goes in v3:
time: 122 us
  Pallas kernels  120 us (98%)
  local copies, waits for them, and re-layouts  1.87 us (2%)
    pallas_call x1, Pallas kernels, body(): pl.pallas_call(functools.partial(kernel, n_genome, n_samp, nb, half, trai...  120 us

profile of v3, /device:TPU:0, one launch (start us, length us, event | category | flops | bytes accessed | tf_op | source)
XLA Modules:
  0.0 121.6 jit_solution(8355679024992777586)
XLA Ops:
  0.0 119.7 %shard_map.37 = f32[1024,128]{1,0:T(8,128)} custom-call(bf16[4096,1024]{1,0:T(8,128)(2,1)} %x_ref.1, bf16[1024,128]{1,0:T(8,128)(2,1)} %e_ref.1, s32[4]{0:T(128)} %depth_ref.1), custom_call_target="tpu_custom_call" | custom-call | flops 10737418240 | bytes 16777216 | tf_op jit(solution)/shard_map/pallas_call | solution.py:383
  119.7 1.9 %copy.5 = f32[1024,128]{1,0:T(8,128)} copy(f32[1024,128]{1,0:T(8,128)} %shard_map.37) | data formatting | bytes 1048576

commit v4 on v3

--- a/solution.py
+++ b/solution.py
@@ -285,9 +285,14 @@
             relay("partner", t - 1)
             relay("own", t - 1)
 
+        if t == nb - 1:
+            x_pair(jnp.int32(t), 0)
+            publish("own", t)
+
         @pl.when(has_from)
         def _():
-            z_copies[t].wait_recv()
+            if t < nb - 1:
+                z_copies[t].wait_recv()
 
             def z_pair(v, carry):
                 k = nb + v - t
@@ -303,23 +308,33 @@
                 lax.fori_loop(0, t + 1, z_pair, 0)
             else:
                 for v in range(nb):
+                    if v == t:
+                        z_copies[t].wait_recv()
                     z_pair(jnp.int32(v), 0)
                     publish("far", v)
-
-        lax.fori_loop(t, nb, x_pair, 0)
+                    if v > 0:
+                        relay("far", v - 1)
+
+        if t < nb - 1:
+            lax.fori_loop(t, nb, x_pair, 0)
         publish("partner", t)
-        publish("own", t)
+        if t < nb - 1:
+            publish("own", t)
         if 0 < t < nb - 1:
             prepare(0, t - 1)
 
     @pl.when(has_from)
     def _():
-        for v in range(nb):
-            relay("far", v)
-
-    forward(0, nb - 2)
+        relay("far", nb - 1)
+
     relay("partner", nb - 1)
     relay("own", nb - 1)
+    forward(0, nb - 2)
+
+    @pl.when(has_from)
+    def _():
+        for v in range(nb - 1):
+            forward(1, v)
 
     loc_across.wait_recv()
     out_ref[...] = loc[:, my_cols] + lc_in[my_y] + ly_in[...]
@@ -328,8 +343,7 @@
 
     @pl.when(has_from)
     def _():
-        for v in range(nb):
-            forward(1, v)
+        forward(1, nb - 1)
 
     forward(0, nb - 1)
     out_ref[rows(mine(nb - 1)), :] += collect("own", nb - 1)

time: 122 us -> 120 us (0.984)
  Pallas kernels: 120 us -> 118 us
    pallas_call x1, Pallas kernels: 120 us -> 118 us  [body(): pl.pallas_call(functools.partial(kernel, n_genome, n_samp, nb, half, trai...]
where the time goes in v4:
time: 120 us
  Pallas kernels  118 us (98%)
  local copies, waits for them, and re-layouts  1.87 us (2%)
    pallas_call x1, Pallas kernels, body(): pl.pallas_call(functools.partial(kernel, n_genome, n_samp, nb, half, trai...  118 us

profile of v4, /device:TPU:0, one launch (start us, length us, event | category | flops | bytes accessed | tf_op | source)
XLA Modules:
  0.0 120.3 jit_solution(13575513131529145387)
XLA Ops:
  0.0 118.4 %shard_map.37 = f32[1024,128]{1,0:T(8,128)} custom-call(bf16[4096,1024]{1,0:T(8,128)(2,1)} %x_ref.1, bf16[1024,128]{1,0:T(8,128)(2,1)} %e_ref.1, s32[4]{0:T(128)} %depth_ref.1), custom_call_target="tpu_custom_call" | custom-call | flops 10737418240 | bytes 16777216 | tf_op jit(solution)/shard_map/pallas_call | solution.py:397
  118.5 1.9 %copy.5 = f32[1024,128]{1,0:T(8,128)} copy(f32[1024,128]{1,0:T(8,128)} %shard_map.37) | data formatting | bytes 1048576
